TPU v7x, 32 devices: a whole 2x2x4 slice. The times are simulated.
32 devices in a mesh: groups: 2 (over y), rows: 8 (over z, core), cols: 2 (over x).
Axes of the slice: x: 2, y: 2, z: 4, core: 2. Of those that a mesh axis runs over, the one named last changes fastest.
Arguments:
- big_emb: bfloat16 [8192, 768], P(('groups', 'rows', 'cols')), parts along dimension 0, may hold values from -6 to 6
- big_order: int32 [8192], P(('groups', 'rows', 'cols')), parts along dimension 0, may hold values from 0 to 4095, each once
- small_emb: bfloat16 [32, 8, 16, 768], P(('groups', 'rows', 'cols')), parts along dimension 0, may hold values from -6 to 6
- small_clus: int32 [32, 8, 16], P(('groups', 'rows', 'cols')), parts along dimension 0, may hold values from -1 to 15, as said below
- small_order: int32 [32, 8, 16], P(('groups', 'rows', 'cols')), parts along dimension 0, may hold values from 0 to 2047, as said below
Outputs:
- big_best: float32 [8192], P(('groups', 'rows', 'cols')), parts along dimension 0
- small_best: float32 [32, 8, 16], P(('groups', 'rows', 'cols')), parts along dimension 0
There are 2 independent parts, one for each index of `groups`. A program takes and returns all parts, laid end to end along the dimension named above; each array names one. Nothing has to cross between parts.
Inputs may be any that keep to these rules, and one draw needn't show every extreme that they name: `small_clus`: -1 marks an empty slot; otherwise one of the 16 clusters of the destination device. The slots to one destination from one source are at most 16 live, and in every draw some source fills all 16 slots to some destination. `small_order`: each value occurs once within each part within each part (each index of `groups`).
All inputs are finite; a program needn't handle non-finite values.
Results may differ from a plain program's by a relative error of at most 0.0012.
Values may be sent and summed in bfloat16 or wider, within the bound.
A program may use at most 64 MiB of HBM per device.

v0:
```python
import jax
import jax.numpy as jnp
from jax import lax
from jax.sharding import PartitionSpec as P


def normalize(values):
    floats = values.astype(jnp.float32)
    squares = jnp.sum(floats * floats, axis=-1, keepdims=True)
    return (floats * lax.rsqrt(squares + 1e-06)).astype(jnp.bfloat16)


def best_over(row_emb, row_ord, col_emb, col_ord):
    total_rows = row_emb.shape[0]
    height = 512

    def one_block(block_at):
        rows_here = lax.dynamic_slice_in_dim(row_emb, block_at * height, height, 0)
        ord_here = lax.dynamic_slice_in_dim(row_ord, block_at * height, height, 0)
        scores = lax.dot_general(
            rows_here, col_emb, (((1,), (1,)), ((), ())), preferred_element_type=jnp.float32
        )
        allowed = col_ord[None, :] < ord_here[:, None]
        return jnp.max(jnp.where(allowed, scores, jnp.float32(-1.0)), axis=1)

    blocks = lax.map(one_block, jnp.arange(total_rows // height, dtype=jnp.int32))
    return jnp.maximum(blocks.reshape(total_rows), jnp.float32(-1.0))


def cluster_best(slots, clusters, orders):
    scores = lax.dot_general(
        slots, slots, (((1,), (1,)), ((), ())), preferred_element_type=jnp.float32
    )
    allowed = (
        (clusters[None, :] == clusters[:, None])
        & (clusters[:, None] >= 0)
        & (orders[None, :] < orders[:, None])
    )
    return jnp.max(jnp.where(allowed, scores, jnp.float32(-1.0)), axis=1)


def local(big_emb, big_order, small_emb, small_clus, small_order):
    own_rows = big_emb.shape[0]
    big_unit = normalize(big_emb)
    small_unit = normalize(small_emb)
    sent_emb, sent_clus, sent_ord = (
        lax.all_to_all(small_unit, "rows", split_axis=1, concat_axis=1, tiled=True),
        lax.all_to_all(small_clus, "rows", split_axis=1, concat_axis=1, tiled=True),
        lax.all_to_all(small_order, "rows", split_axis=1, concat_axis=1, tiled=True),
    )
    depth = sent_emb.shape[1] * sent_emb.shape[2]
    slot_best = cluster_best(
        sent_emb.reshape(depth, sent_emb.shape[3]),
        sent_clus.reshape(depth),
        sent_ord.reshape(depth),
    )
    slot_best = slot_best.reshape(sent_clus.shape)
    row_emb, row_ord = (
        lax.all_gather(big_unit, "cols", axis=0, tiled=True),
        lax.all_gather(big_order, "cols", axis=0, tiled=True),
    )
    initial = jnp.full((row_emb.shape[0],), -1.0, jnp.float32)
    partial_value = jnp.maximum(
        initial,
        best_over(
            row_emb,
            row_ord,
            lax.all_gather(big_unit, "rows", axis=0, tiled=True),
            lax.all_gather(big_order, "rows", axis=0, tiled=True),
        ),
    )
    merged = lax.pmax(partial_value, "cols")
    big_best = lax.dynamic_slice_in_dim(merged, lax.axis_index("cols") * own_rows, own_rows, 0)
    small_best = lax.all_to_all(slot_best, "rows", split_axis=1, concat_axis=1, tiled=True)
    return (big_best, small_best)


def solution(mesh):
    placed = (
        P(("groups", "rows", "cols"), None),
        P(("groups", "rows", "cols")),
        P(("groups", "rows", "cols"), None, None, None),
        P(("groups", "rows", "cols"), None, None),
        P(("groups", "rows", "cols"), None, None),
    )
    return jax.shard_map(
        local,
        mesh=mesh,
        in_specs=placed,
        out_specs=(P(("groups", "rows", "cols")), P(("groups", "rows", "cols"), None, None)),
        check_vma=False,
    )
```

profile of v0, /device:TPU:0, one launch (start us, length us, event | category | flops | bytes accessed | tf_op | source)
XLA Modules:
  0.0 83.8 jit_solution(2112146091441584456)
XLA Ops:
  7.2 1.2 %fusion.1 = f32[256]{0:T(256)S(1)} fusion(bf16[256,768]{1,0:T(8,128)(2,1)} %param.5), kind=kLoop, calls=%fused_computation.5 | loop fusion | flops 589568 | bytes 394240 | tf_op jit(solution)/shard_map/reduce_sum | solution.py:9
  8.4 1.9 %fusion.2 = bf16[256,768]{1,0:T(8,128)(2,1)} fusion(bf16[256,768]{1,0:T(8,128)(2,1)} %param.5, f32[256]{0:T(256)S(1)} %add_rsqrt_fusion.1), kind=kLoop, calls=%fused_computation.6 | loop fusion | flops 589824 | bytes 787456 | tf_op jit(solution)/shard_map/convert_element_type | solution.py:10
  10.3 6.4 %all-to-all-start.1 = ((s32[1,8,16]{2,0,1:T(1,128)}), s32[1,8,16]{2,0,1:T(1,128)S(1)}, u32[]{:S(2)}, u32[]{:S(2)}) async-start(s32[1,8,16]{2,0,1:T(1,128)} %bitcast.22), calls=%async_computation.1 | async-start | bytes 8192 | tf_op jit(solution)/shard_map/all_to_all | solution.py:49
  16.6 1.0 %fusion.3 = f32[8,16]{1,0:T(8,128)S(1)} fusion(bf16[1,8,16,768]{3,2,1,0:T(8,128)(2,1)} %param.7), kind=kLoop, calls=%fused_computation.9 | loop fusion | flops 294784 | bytes 197120 | tf_op jit(solution)/shard_map/reduce_sum | solution.py:9
  17.7 1.7 %fusion.4 = bf16[1,8,16,768]{3,2,0,1:T(8,128)(2,1)} fusion(bf16[1,8,16,768]{3,2,1,0:T(8,128)(2,1)} %param.7, f32[8,16]{1,0:T(8,128)S(1)} %add_rsqrt_fusion), kind=kLoop, calls=%fused_computation.10 | loop fusion | flops 294912 | bytes 393728 | tf_op jit(solution)/shard_map/convert_element_type | solution.py:10
  19.4 2.7 %all-to-all-done.1 = s32[1,8,16]{2,0,1:T(1,128)S(1)} async-done(((s32[1,8,16]{2,0,1:T(1,128)}), s32[1,8,16]{2,0,1:T(1,128)S(1)}, u32[]{:S(2)}, u32[]{:S(2)}) %all-to-all-start.1) | async-done | bytes 544 | tf_op jit(solution)/shard_map/all_to_all | solution.py:49
  22.1 3.3 %all-to-all-start = ((s32[1,8,16]{2,0,1:T(1,128)}), s32[1,8,16]{2,0,1:T(1,128)S(1)}, u32[]{:S(2)}, u32[]{:S(2)}) async-start(s32[1,8,16]{2,0,1:T(1,128)} %bitcast.23), calls=%async_computation | async-start | bytes 8192 | tf_op jit(solution)/shard_map/all_to_all | solution.py:48
  25.4 12.6 %all-gather = s32[8,1,256]{2,1,0:T(1,128)S(1)} all-gather(s32[1,1,256]{2,1,0:T(1,128)} %bitcast.20), channel_id=1, replica_groups=mesh['groups'=2,'rows'=8,'cols'=2] {'rows'}, dimensions={0}, use_global_device_ids=true | all-gather | bytes 9216 | tf_op jit(solution)/shard_map/all_gather | solution.py:69
  38.0 3.4 %all-to-all-start.2 = ((bf16[1,8,16,768]{3,2,0,1:T(8,128)(2,1)}), bf16[1,8,16,768]{3,2,0,1:T(8,128)(2,1)S(1)}, u32[]{:S(2)}, u32[]{:S(2)}) async-start(bf16[1,8,16,768]{3,2,0,1:T(8,128)(2,1)} %fusion.4), calls=%async_computation.2 | async-start | bytes 393216 | tf_op jit(solution)/shard_map/all_to_all | solution.py:47
  41.4 12.3 %all_gather.14 = bf16[512,768]{1,0:T(8,128)(2,1)S(1)} all-gather(bf16[256,768]{1,0:T(8,128)(2,1)} %fusion.2), channel_id=1, replica_groups=mesh['groups'=2,'rows'=8,'cols'=2] {'cols'}, dimensions={0}, use_global_device_ids=true | all-gather | bytes 1179648 | tf_op jit(solution)/shard_map/all_gather | solution.py:59
  53.7 0.5 broadcast.29
  54.2 0.7 reduce.7
  54.9 0.1 lt.46
  55.0 0.7 reduce.8
  55.6 0.1 eq.15
  55.7 0.2 fusion
  56.0 0.7 reshape.43
  56.7 4.8 %all-to-all-start.3 = ((f32[1,8,16]{2,0,1:T(1,128)}), f32[1,8,16]{2,0,1:T(1,128)S(1)}, u32[]{:S(2)}, u32[]{:S(2)}) async-start(f32[1,8,16]{2,0,1:T(1,128)} %bitcast.7), calls=%async_computation.3 | async-start | bytes 8192 | tf_op jit(solution)/shard_map/all_to_all | solution.py:74
  61.4 4.2 %all-gather.1 = s32[2,1,256]{2,1,0:T(1,128)S(1)} all-gather(s32[1,1,256]{2,1,0:T(1,128)S(1)} %bitcast.21), channel_id=1, replica_groups=mesh['groups'=2,'rows'=8,'cols'=2] {'cols'}, dimensions={0}, use_global_device_ids=true | all-gather | bytes 3072 | tf_op jit(solution)/shard_map/all_gather | solution.py:60
  65.7 1.2 %all-to-all-done.3 = f32[1,8,16]{2,0,1:T(1,128)S(1)} async-done(((f32[1,8,16]{2,0,1:T(1,128)}), f32[1,8,16]{2,0,1:T(1,128)S(1)}, u32[]{:S(2)}, u32[]{:S(2)}) %all-to-all-start.3) | async-done | bytes 544 | tf_op jit(solution)/shard_map/all_to_all | solution.py:74
  66.9 3.8 %select_reduce_fusion = f32[512]{0:T(512)S(1)} fusion(bf16[512,768]{1,0:T(8,128)(2,1)S(1)} %all_gather.14, bf16[2048,768]{1,0:T(8,128)(2,1)} %all-gather.4.cloned.1.call-done, s32[2048]{0:T(1024)S(1)} %bitcast.19, s32[512]{0:T(512)S(1)} %bitcast.24), kind=kOutput, calls=%fused_computation | convolution fusion | flops 1613757952 | bytes 3944448 | tf_op jit(solution)/shard_map/while/body/eval_jaxpr/dot_general | solution.py:20
  70.8 4.9 %pmax.7 = f32[512]{0:T(512)S(1)} all-reduce(f32[512]{0:T(512)S(1)} %broadcast_maximum_fusion), channel_id=1, replica_groups=mesh['groups'=2,'rows'=8,'cols'=2] {'cols'}, use_global_device_ids=true, to_apply=%region_2.3 | all-reduce | flops 512 | bytes 4096 | tf_op jit(solution)/shard_map/pmax | solution.py:72
  75.7 0.6 dynamic_slice.10
  76.3 0.6 copy.18
  (11 shorter events, 0.1 us)
Async XLA Ops:
  7.2 54.3 %copy-start = (s32[256]{0:T(256)S(1)}, s32[256]{0:T(256)}, u32[]{:S(2)}) copy-start(s32[256]{0:T(256)} %param.6) | copy-start | bytes 3076
  7.2 59.7 %all-gather.4.cloned.1.call-start = ((), (), s32[]{:S(2)}) async-start(), calls=%async_computation.4 | async-start | bytes 3538944 | tf_op jit(solution)/shard_map/all_gather | solution.py:68
  10.3 11.8 %all-to-all-start.1 = ((s32[1,8,16]{2,0,1:T(1,128)}), s32[1,8,16]{2,0,1:T(1,128)S(1)}, u32[]{:S(2)}, u32[]{:S(2)}) async-start(s32[1,8,16]{2,0,1:T(1,128)} %bitcast.22), calls=%async_computation.1 | async-start | bytes 8192 | tf_op jit(solution)/shard_map/all_to_all | solution.py:49
  22.1 15.9 %all-to-all-start = ((s32[1,8,16]{2,0,1:T(1,128)}), s32[1,8,16]{2,0,1:T(1,128)S(1)}, u32[]{:S(2)}, u32[]{:S(2)}) async-start(s32[1,8,16]{2,0,1:T(1,128)} %bitcast.23), calls=%async_computation | async-start | bytes 8192 | tf_op jit(solution)/shard_map/all_to_all | solution.py:48
  38.0 17.7 %all-to-all-start.2 = ((bf16[1,8,16,768]{3,2,0,1:T(8,128)(2,1)}), bf16[1,8,16,768]{3,2,0,1:T(8,128)(2,1)S(1)}, u32[]{:S(2)}, u32[]{:S(2)}) async-start(bf16[1,8,16,768]{3,2,0,1:T(8,128)(2,1)} %fusion.4), calls=%async_computation.2 | async-start | bytes 393216 | tf_op jit(solution)/shard_map/all_to_all | solution.py:47
  56.7 10.3 %all-to-all-start.3 = ((f32[1,8,16]{2,0,1:T(1,128)}), f32[1,8,16]{2,0,1:T(1,128)S(1)}, u32[]{:S(2)}, u32[]{:S(2)}) async-start(f32[1,8,16]{2,0,1:T(1,128)} %bitcast.7), calls=%async_computation.3 | async-start | bytes 8192 | tf_op jit(solution)/shard_map/all_to_all | solution.py:74
Sparse Core Ops, SparseCore 0:
  10.4 45.3 all-gather.3
where the time goes:
time: 84.3 us; the launch traced here: 83.8 us
  blocking collectives  34.1 us (40%)
  starting transfers between devices  17.9 us (21%)
  between operations  14.1 us (17%)
  other arithmetic  7.12 us (8%)
  matrix products  4.07 us (5%)
  waiting for transfers between devices  3.99 us (5%)
  local copies, waits for them, and re-layouts  2.59 us (3%)
    all_gather x1, blocking collectives, local(): lax.all_gather(big_order, 'rows', axis=0, tiled=True)  12.6 us
    all_gather x1, blocking collectives, local(): lax.all_gather(big_unit, 'cols', axis=0, tiled=True)  12.3 us
    all_to_all x1, starting transfers between devices, local(): lax.all_to_all(small_order, 'rows', split_axis=1, concat_axis=1, tiled=True)  6.36 us
    pmax x1, blocking collectives, local(): merged = lax.pmax(partial_value, 'cols')  4.94 us
    all_to_all x1, starting transfers between devices, local(): lax.all_to_all(slot_best, 'rows', split_axis=1, concat_axis=1, tiled=True)  4.78 us
    all_gather x1, blocking collectives, local(): lax.all_gather(big_order, 'cols', axis=0, tiled=True)  4.25 us
    dot_general x1, matrix products, one_block(): lax.dot_general(rows_here, col_emb, (((1,), (1,)), ((), ())), preferred_e...  3.83 us
    convert_element_type x2, other arithmetic, normalize(): return (floats * lax.rsqrt(squares + 1e-06)).astype(jnp.bfloat16)  3.57 us
  transfers between devices with their start and end apart: 5, of which 2 were waited for; matrix products, arithmetic and copies ran while one was open for 7% of the time, Pallas kernels for 0%

commit v1 on v0

v1 whole, which is shorter than its diff:
```python
import functools

import jax
import jax.numpy as jnp
from jax import lax
from jax.experimental import pallas as pl
from jax.experimental.pallas import tpu as pltpu
from jax.sharding import PartitionSpec as P

LANES = 128
MESH = pl.DeviceIdType.MESH


def normalize(values):
    floats = values.astype(jnp.float32)
    squares = jnp.sum(floats * floats, axis=-1, keepdims=True)
    return (floats * lax.rsqrt(squares + 1e-06)).astype(jnp.bfloat16)


def upright(row):
    return jnp.broadcast_to(row, (LANES, LANES)).T


def kernel(
    n_rows, n_cols,
    be, bo, se, sc, so, out_b, out_s,
    col_buf, row_buf, row_ord, meta_s, meta_r, sm_s, sm_r, acc, pm_s, pm_r, cm_s, cm_r, rs_s, rs_r, pad,
    recv, up_sem, down_sem, core_sem, x_send, x_recv, xo_send, xo_recv,
    me_send, me_recv, sm_send, sm_recv, rs_send, rs_recv, pm_send, pm_recv, cm_send, cm_recv,
):
    r = lax.axis_index("rows")
    c = lax.axis_index("cols")
    z, core = r // 2, r % 2
    partner = z * 2 + 1 - core
    depth, half = n_rows // 2, n_rows // 4
    block = be.shape[0]
    chunks = block // LANES
    cap = se.shape[2]
    width = rs_s.shape[1]

    def peers(count, me, body):
        def one(d, carry):
            body(lax.rem(me + d, count))
            return carry
        lax.fori_loop(1, count, one, 0)

    barrier = pltpu.get_barrier_semaphore()
    peers(n_rows, r, lambda p: pl.semaphore_signal(barrier, inc=1, device_id={"rows": p}, device_id_type=MESH))
    peers(n_cols, c, lambda p: pl.semaphore_signal(barrier, inc=1, device_id={"cols": p}, device_id_type=MESH))

    def remote(src, dst, send, recv_sem, axis, to):
        return pltpu.make_async_remote_copy(
            src_ref=src, dst_ref=dst, send_sem=send, recv_sem=recv_sem, device_id={axis: to}, device_id_type=MESH
        )

    def part(b, k):
        return col_buf.at[b, pl.ds(k * LANES, LANES), :]

    def hop(b, k, sems, to):
        return remote(part(b, k), part(b, k), sems.at[b // 2, k], recv.at[b, k], "rows", to)

    def x_copy(k, to, owner):
        lines = pl.ds(k * LANES, LANES)
        return remote(part(r, k), row_buf.at[owner, lines, :], x_send.at[to, k], x_recv.at[owner, k], "cols", to)

    def xo_copy(to, owner):
        return remote(bo, row_ord.at[owner], xo_send.at[to], xo_recv.at[owner], "cols", to)

    def me_copy(to, owner):
        return remote(meta_s.at[to], meta_r.at[owner], me_send.at[to], me_recv.at[owner], "rows", to)

    def sm_copy(to, owner):
        return remote(sm_s.at[to], sm_r.at[owner], sm_send.at[to], sm_recv.at[owner], "rows", to)

    def rs_copy(to, owner):
        return remote(rs_s, rs_r.at[owner], rs_send.at[to], rs_recv.at[owner], "rows", to)

    def pm_copy(to, owner):
        return remote(pm_s.at[to], pm_r.at[owner], pm_send.at[to], pm_recv.at[owner], "cols", to)

    def cm_copy(to, owner):
        return remote(cm_s.at[to], cm_r.at[owner], cm_send.at[to], cm_recv.at[owner], "rows", to)

    def below_ok(s):
        return (z - s >= 0) & (z - s < half)

    def above_ok(s):
        return (z + s < depth) & (z >= half)

    for k in range(chunks):
        lines = pl.ds(k * LANES, LANES)
        unit = normalize(be[lines, :])
        col_buf[r, lines, :] = unit
        row_buf[c, lines, :] = unit
        if k == 0:
            pl.semaphore_wait(barrier, n_rows - 1 + n_cols - 1)

        @pl.when(z < half)
        def _():
            hop(r, k, up_sem, r + 2).start()

        @pl.when(z > half)
        def _():
            hop(r, k, down_sem, r - 2).start()

        hop(r, k, core_sem, partner).start()
        peers(n_cols, c, lambda p: x_copy(k, p, c).start())

    row_ord[c] = bo[...]
    peers(n_cols, c, lambda p: xo_copy(p, c).start())

    pad[...] = jnp.zeros_like(pad)
    pad[0, :, :cap] = sc[0]
    pad[1, :, :cap] = so[0]
    clus = pltpu.roll(pad[0], r * cap, 1)
    order = pltpu.roll(pad[1], r * cap, 1)
    for p in range(n_rows):
        meta_s[p, 0:1, :block] = bo[...]
        meta_s[p, 1:2, :width] = clus[p:p + 1, :]
        meta_s[p, 2:3, :width] = order[p:p + 1, :]
    peers(n_rows, r, lambda p: me_copy(p, r).start())
    sm_s[...] = normalize(se[0])
    peers(n_rows, r, lambda p: sm_copy(p, r).start())
    meta_r[r] = meta_s[r]
    sm_r[r] = sm_s[r]
    acc[...] = jnp.full(acc.shape, -1.0, jnp.float32)

    def forward(s, k):
        @pl.when(below_ok(s))
        def _():
            b = r - 2 * s
            hop(b, k, core_sem, partner).wait_recv()

            @pl.when(z < depth - 1)
            def _():
                hop(b, k, up_sem, r + 2).start()

            hop(b, k, core_sem, partner).start()

        @pl.when(above_ok(s))
        def _():
            b = r + 2 * s
            hop(b, k, core_sem, partner).wait_recv()

            @pl.when(z > half)
            def _():
                hop(b, k, down_sem, r - 2).start()

            hop(b, k, core_sem, partner).start()

    def scores_of(b, k, both):
        at = pl.ds(k * LANES, LANES)
        ord_col = upright(meta_r[b, 0:1, at])
        rows = row_buf[...].reshape(n_cols * block, row_buf.shape[2])
        scores = lax.dot_general(
            col_buf[b, at, :], rows, (((1,), (1,)), ((), ())), preferred_element_type=jnp.float32
        )
        best = jnp.full((LANES, LANES), -1.0, jnp.float32)
        for tile in range(n_cols * block // LANES):
            lanes = slice(tile * LANES, (tile + 1) * LANES)
            here = scores[:, lanes]
            lane = (tile * LANES) % block
            ord_row = row_ord[tile * LANES // block, 0:1, lane:lane + LANES]
            kept = jnp.where(ord_col < ord_row, here, jnp.float32(-1.0))
            acc[:, lanes] = jnp.maximum(acc[:, lanes], jnp.max(kept.reshape(LANES // 8, 8, LANES), axis=0))
            if both:
                best = jnp.maximum(best, jnp.where(ord_row < ord_col, here, jnp.float32(-1.0)))
        if both:
            cm_s[b, 0:1, at] = jnp.max(best.T, axis=0, keepdims=True)

    def pair(b, k):
        other = (b // 2) * 2 + 1 - core
        hop(other, k, core_sem, partner).wait_recv()
        scores_of(b, k, True)
        scores_of(other, k, True)
        if k == chunks - 1:
            cm_copy(b, r).start()
            cm_copy(other, r).start()

    def pairs(s, k):
        @pl.when(below_ok(s))
        def _():
            pair(r - 2 * s, k)

        @pl.when(above_ok(s))
        def _():
            pair(r + 2 * s, k)

    if depth > 1:
        for k in range(chunks):
            forward(1, k)
    for k in range(chunks):
        peers(n_cols, c, lambda p: x_copy(k, p, p).wait_recv())
    peers(n_cols, c, lambda p: xo_copy(p, p).wait_recv())
    peers(n_rows, r, lambda p: me_copy(p, p).wait_recv())
    for k in range(chunks):
        scores_of(r, k, False)
        hop(partner, k, core_sem, partner).wait_recv()
        scores_of(partner, k, False)

    peers(n_rows, r, lambda p: sm_copy(p, p).wait_recv())
    slots = n_rows * cap
    clus_row = jnp.sum(meta_r[:, 1, :width], axis=0, keepdims=True)
    ord_row = jnp.sum(meta_r[:, 2, :width], axis=0, keepdims=True)
    emb = sm_r[...].reshape(slots, sm_r.shape[2])
    best = jnp.full((1, width), -1.0, jnp.float32)
    for at in range(0, slots, LANES):
        scores = lax.dot_general(
            emb[at:at + LANES], emb, (((1,), (1,)), ((), ())), preferred_element_type=jnp.float32
        )
        clus_col = jnp.broadcast_to(upright(clus_row[:, at:at + LANES])[:, :1], (LANES, width))
        ord_col = jnp.broadcast_to(upright(ord_row[:, at:at + LANES])[:, :1], (LANES, width))
        allowed = (clus_col == clus_row) & (clus_row >= 0) & (ord_col < ord_row)
        kept = jnp.where(allowed, scores, jnp.float32(-1.0))
        best = jnp.maximum(best, jnp.max(kept, axis=0, keepdims=True))
    rs_s[...] = best
    rs_r[r] = best
    peers(n_rows, r, lambda p: rs_copy(p, r).start())

    def step(s, carry):
        for k in range(chunks):
            forward(s, k)
            pairs(s - 1, k)
        return carry

    lax.fori_loop(2, depth, step, 0)
    for k in range(chunks):
        pairs(depth - 1, k)

    final = jnp.max(acc[...], axis=0, keepdims=True)
    for p in range(n_cols):
        pm_s[p] = final[:, p * block:(p + 1) * block]
    peers(n_cols, c, lambda p: pm_copy(p, c).start())

    peers(n_rows, r, lambda p: rs_copy(p, p).wait_recv())
    back = pltpu.roll(rs_r[:, 0, :], lax.rem(width - r * cap, width), 1)
    out_s[0] = back[:, :cap]

    out_b[...] = pm_s[c]

    def returned(p, carry):
        zp = p // 2
        low = (z < half) & (zp > z)
        high = (z >= half) & (zp >= half) & (zp < z)

        @pl.when(low | high)
        def _():
            cm_copy(p, p).wait_recv()
            out_b[...] = jnp.maximum(out_b[...], cm_r[p])
        return carry

    lax.fori_loop(0, n_rows, returned, 0)

    def merge(p):
        pm_copy(p, p).wait_recv()
        out_b[...] = jnp.maximum(out_b[...], pm_r[p])

    peers(n_cols, c, merge)

    def sent(b):
        for k in range(chunks):
            hop(b, k, core_sem, partner).wait_send()

    for k in range(chunks):
        hop(r, k, core_sem, partner).wait_send()

        @pl.when(z < half)
        def _():
            hop(r, k, up_sem, r + 2).wait_send()

        @pl.when(z > half)
        def _():
            hop(r, k, down_sem, r - 2).wait_send()

        peers(n_cols, c, lambda p: x_copy(k, p, c).wait_send())

    def drained(s, carry):
        @pl.when(below_ok(s))
        def _():
            b = r - 2 * s
            sent(b)
            cm_copy(b, r).wait_send()
            cm_copy((b // 2) * 2 + 1 - core, r).wait_send()

            @pl.when(z < depth - 1)
            def _():
                for k in range(chunks):
                    hop(b, k, up_sem, r + 2).wait_send()

        @pl.when(above_ok(s))
        def _():
            b = r + 2 * s
            sent(b)
            cm_copy(b, r).wait_send()
            cm_copy((b // 2) * 2 + 1 - core, r).wait_send()

            @pl.when(z > half)
            def _():
                for k in range(chunks):
                    hop(b, k, down_sem, r - 2).wait_send()
        return carry

    lax.fori_loop(1, depth, drained, 0)

    def row_sent(p):
        me_copy(p, r).wait_send()
        sm_copy(p, r).wait_send()
        rs_copy(p, r).wait_send()

    peers(n_rows, r, row_sent)

    def col_sent(p):
        xo_copy(p, c).wait_send()
        pm_copy(p, c).wait_send()

    peers(n_cols, c, col_sent)


def local(n_rows, n_cols, big_emb, big_order, small_emb, small_clus, small_order):
    block, dim = big_emb.shape
    cap = small_emb.shape[2]
    width = n_rows * cap
    chunks = block // LANES
    depth = n_rows // 2
    meta = max(block, width)
    bf16, f32, i32 = jnp.bfloat16, jnp.float32, jnp.int32
    dma = pltpu.SemaphoreType.DMA
    vmem = pl.BlockSpec(memory_space=pltpu.VMEM)
    big, small = pl.pallas_call(
        functools.partial(kernel, n_rows, n_cols),
        out_shape=(
            jax.ShapeDtypeStruct((1, block), f32),
            jax.ShapeDtypeStruct((1, n_rows, cap), f32),
        ),
        in_specs=[vmem] * 5,
        out_specs=(vmem, vmem),
        scratch_shapes=[
            pltpu.VMEM((n_rows, block, dim), bf16),
            pltpu.VMEM((n_cols, block, dim), bf16),
            pltpu.VMEM((n_cols, 1, block), i32),
            pltpu.VMEM((n_rows, 8, meta), i32),
            pltpu.VMEM((n_rows, 8, meta), i32),
            pltpu.VMEM((n_rows, cap, dim), bf16),
            pltpu.VMEM((n_rows, cap, dim), bf16),
            pltpu.VMEM((8, n_cols * block), f32),
            pltpu.VMEM((n_cols, 1, block), f32),
            pltpu.VMEM((n_cols, 1, block), f32),
            pltpu.VMEM((n_rows, 1, block), f32),
            pltpu.VMEM((n_rows, 1, block), f32),
            pltpu.VMEM((1, width), f32),
            pltpu.VMEM((n_rows, 1, width), f32),
            pltpu.VMEM((2, n_rows, width), i32),
            dma((n_rows, chunks)),
            dma((depth, chunks)),
            dma((depth, chunks)),
            dma((depth, chunks)),
            dma((n_cols, chunks)),
            dma((n_cols, chunks)),
            dma((n_cols,)),
            dma((n_cols,)),
            dma((n_rows,)),
            dma((n_rows,)),
            dma((n_rows,)),
            dma((n_rows,)),
            dma((n_rows,)),
            dma((n_rows,)),
            dma((n_cols,)),
            dma((n_cols,)),
            dma((n_rows,)),
            dma((n_rows,)),
        ],
        compiler_params=pltpu.CompilerParams(
            collective_id=0, has_side_effects=True, vmem_limit_bytes=48 * 1024 * 1024
        ),
    )(big_emb, big_order.reshape(1, block), small_emb, small_clus, small_order)
    return big.reshape(block), small


def solution(mesh):
    placed = (
        P(("groups", "rows", "cols"), None),
        P(("groups", "rows", "cols")),
        P(("groups", "rows", "cols"), None, None, None),
        P(("groups", "rows", "cols"), None, None),
        P(("groups", "rows", "cols"), None, None),
    )
    return jax.shard_map(
        functools.partial(local, mesh.shape["rows"], mesh.shape["cols"]),
        mesh=mesh,
        in_specs=placed,
        out_specs=(P(("groups", "rows", "cols")), P(("groups", "rows", "cols"), None, None)),
        check_vma=False,
    )
```

time: 84.3 us -> 48.1 us (0.57)
  Pallas kernels: 0 us -> 42 us
  blocking collectives: 34.1 us -> 0 us
  starting transfers between devices: 17.9 us -> 0 us
  between operations: 14.1 us -> 0.65 us
  other arithmetic: 7.12 us -> 0 us
  matrix products: 4.07 us -> 0 us
  waiting for transfers between devices: 3.99 us -> 0 us
  local copies, waits for them, and re-layouts: 2.59 us -> 5.12 us
    pallas_call x0 -> x1, Pallas kernels: none -> 42 us  [local(): pl.pallas_call(functools.partial(kernel, n_rows, n_cols), out_shape=(jax....]
    all_gather x3 -> x0, blocking collectives: 29.1 us -> none  [the longest x1 12.6 us: local(): lax.all_gather(big_order, 'rows', axis=0, tiled=True)]
    all_to_all x4 -> x0, starting transfers between devices: 17.8 us -> none  [the longest x1 6.36 us: local(): lax.all_to_all(small_order, 'rows', split_axis=1, concat_axis=1, tiled=True)]
    pmax x1 -> x0, blocking collectives: 4.94 us -> none  [local(): merged = lax.pmax(partial_value, 'cols')]
    unnamed x3 -> x12, local copies, waits for them, and re-layouts: 0.6 us -> 5.12 us
    dot_general x2 -> x0, matrix products: 4.07 us -> none  [the longest x1 3.83 us: one_block(): lax.dot_general(rows_here, col_emb, (((1,), (1,)), ((), ())), preferred_e...]
    all_to_all x4 -> x0, waiting for transfers between devices: 3.97 us -> none  [the longest x1 2.73 us: local(): lax.all_to_all(small_order, 'rows', split_axis=1, concat_axis=1, tiled=True)]
    convert_element_type x2 -> x0, other arithmetic: 3.57 us -> none  [normalize(): return (floats * lax.rsqrt(squares + 1e-06)).astype(jnp.bfloat16)]
  transfers between devices with their start and end apart: 5 -> 0, of which waited for: 2 -> 0; matrix products, arithmetic and copies ran while one was open for 7% -> 0% of each run, Pallas kernels for 0% -> 0%
where the time goes in v1:
time: 48.1 us; the launch traced here: 47.8 us
  Pallas kernels  42 us (87%)
  local copies, waits for them, and re-layouts  5.12 us (11%)
  between operations  0.65 us (1%)
    pallas_call x1, Pallas kernels, local(): pl.pallas_call(functools.partial(kernel, n_rows, n_cols), out_shape=(jax....  42 us
    unnamed x12, local copies, waits for them, and re-layouts  5.12 us

profile of v1, /device:TPU:0, one launch (start us, length us, event | category | flops | bytes accessed | tf_op | source)
XLA Modules:
  0.0 47.8 jit_solution(13021644354084956576)
XLA Ops:
  0.6 0.0 copy-start.4
  0.6 0.7 %copy-done.4 = s32[256]{0:T(256)S(1)} copy-done((s32[256]{0:T(256)S(1)}, s32[256]{0:T(256)}, u32[]{:S(2)}) %copy-start.4) | copy-done | bytes 1048
  1.3 0.0 copy-start
  1.3 1.0 %copy-done = bf16[256,768]{1,0:T(8,128)(2,1)S(1)} copy-done((bf16[256,768]{1,0:T(8,128)(2,1)S(1)}, bf16[256,768]{1,0:T(8,128)(2,1)}, u32[]{:S(2)}) %copy-start) | copy-done | bytes 393240
  2.3 0.0 copy-start.1
  2.3 0.9 %copy-done.1 = bf16[1,8,16,768]{3,2,1,0:T(8,128)(2,1)S(1)} copy-done((bf16[1,8,16,768]{3,2,1,0:T(8,128)(2,1)S(1)}, bf16[1,8,16,768]{3,2,1,0:T(8,128)(2,1)}, u32[]{:S(2)}) %copy-start.1) | copy-done | bytes 196632
  3.2 0.0 copy-start.2
  3.2 0.7 %copy-done.2 = s32[1,8,16]{2,1,0:T(8,128)S(1)} copy-done((s32[1,8,16]{2,1,0:T(8,128)S(1)}, s32[1,8,16]{2,1,0:T(8,128)}, u32[]{:S(2)}) %copy-start.2) | copy-done | bytes 536
  3.9 0.0 copy-start.3
  3.9 0.7 %copy-done.3 = s32[1,8,16]{2,1,0:T(8,128)S(1)} copy-done((s32[1,8,16]{2,1,0:T(8,128)S(1)}, s32[1,8,16]{2,1,0:T(8,128)}, u32[]{:S(2)}) %copy-start.3) | copy-done | bytes 536
  4.6 42.0 %shard_map.68 = (f32[1,256]{1,0:T(1,128)S(1)}, f32[1,8,16]{2,1,0:T(8,128)S(1)}) custom-call(bf16[256,768]{1,0:T(8,128)(2,1)S(1)} %copy-done, s32[1,256]{1,0:T(1,128)S(1)} %bitcast.2, bf16[1,8,16,768]{3,2,1,0:T(8,128)(2,1)S(1)} %copy-done.1, s32[1,8,16]{2,1,0:T(8,128)S(1)} %copy-done.2, s32[1,8,16]{2,1,0:T(8,128)S(1)} %copy-done.3), custom_call_target="tpu_custom_call" | custom-call | tf_op jit(solution)/shard_map/pallas_call | solution.py:329
  46.6 0.6 %copy.9 = f32[256]{0:T(256)} copy(f32[256]{0:T(256)S(1)} %bitcast.3) | data formatting | bytes 2048
  47.2 0.6 %copy.10 = f32[1,8,16]{2,1,0:T(8,128)} copy(f32[1,8,16]{2,1,0:T(8,128)S(1)} %get-tuple-element.9) | data formatting | bytes 1024
Async XLA Ops:
  0.6 0.7 %copy-start.4 = (s32[256]{0:T(256)S(1)}, s32[256]{0:T(256)}, u32[]{:S(2)}) copy-start(s32[256]{0:T(256)} %param.6) | copy-start | bytes 3076
  1.3 1.0 %copy-start = (bf16[256,768]{1,0:T(8,128)(2,1)S(1)}, bf16[256,768]{1,0:T(8,128)(2,1)}, u32[]{:S(2)}) copy-start(bf16[256,768]{1,0:T(8,128)(2,1)} %be.1) | copy-start | bytes 1179652
  2.3 0.9 %copy-start.1 = (bf16[1,8,16,768]{3,2,1,0:T(8,128)(2,1)S(1)}, bf16[1,8,16,768]{3,2,1,0:T(8,128)(2,1)}, u32[]{:S(2)}) copy-start(bf16[1,8,16,768]{3,2,1,0:T(8,128)(2,1)} %se.1) | copy-start | bytes 589828
  3.2 0.7 %copy-start.2 = (s32[1,8,16]{2,1,0:T(8,128)S(1)}, s32[1,8,16]{2,1,0:T(8,128)}, u32[]{:S(2)}) copy-start(s32[1,8,16]{2,1,0:T(8,128)} %sc.1) | copy-start | bytes 1540
  3.9 0.7 %copy-start.3 = (s32[1,8,16]{2,1,0:T(8,128)S(1)}, s32[1,8,16]{2,1,0:T(8,128)}, u32[]{:S(2)}) copy-start(s32[1,8,16]{2,1,0:T(8,128)} %so.1) | copy-start | bytes 1540

commit v2 on v1

--- a/solution.py
+++ b/solution.py
@@ -8,6 +8,7 @@
 from jax.sharding import PartitionSpec as P
 
 LANES = 128
+PIECE = 64
 MESH = pl.DeviceIdType.MESH
 
 
@@ -23,18 +24,25 @@
 
 def kernel(
     n_rows, n_cols,
-    be, bo, se, sc, so, out_b, out_s,
-    col_buf, row_buf, row_ord, meta_s, meta_r, sm_s, sm_r, acc, pm_s, pm_r, cm_s, cm_r, rs_s, rs_r, pad,
+    be_in, bo_in, se_in, sc_in, so_in, out_b, out_s,
+    be, bo, se, sc, so, in_sem, col_buf, row_buf, row_ord, meta_s, meta_r, sm_s, sm_r, acc, pm_s, pm_r, cm_s, cm_r, rs_s, rs_r, pad,
     recv, up_sem, down_sem, core_sem, x_send, x_recv, xo_send, xo_recv,
     me_send, me_recv, sm_send, sm_recv, rs_send, rs_recv, pm_send, pm_recv, cm_send, cm_recv,
 ):
+    fetches = [
+        pltpu.make_async_copy(src, dst, in_sem.at[at])
+        for at, (src, dst) in enumerate(((be_in, be), (bo_in, bo), (sc_in, sc), (so_in, so), (se_in, se)))
+    ]
+    for fetch in fetches:
+        fetch.start()
     r = lax.axis_index("rows")
     c = lax.axis_index("cols")
     z, core = r // 2, r % 2
     partner = z * 2 + 1 - core
     depth, half = n_rows // 2, n_rows // 4
     block = be.shape[0]
-    chunks = block // LANES
+    chunks = block // PIECE
+    ratio = LANES // PIECE
     cap = se.shape[2]
     width = rs_s.shape[1]
 
@@ -54,13 +62,13 @@
         )
 
     def part(b, k):
-        return col_buf.at[b, pl.ds(k * LANES, LANES), :]
+        return col_buf.at[b, pl.ds(k * PIECE, PIECE), :]
 
     def hop(b, k, sems, to):
         return remote(part(b, k), part(b, k), sems.at[b // 2, k], recv.at[b, k], "rows", to)
 
     def x_copy(k, to, owner):
-        lines = pl.ds(k * LANES, LANES)
+        lines = pl.ds(k * PIECE, PIECE)
         return remote(part(r, k), row_buf.at[owner, lines, :], x_send.at[to, k], x_recv.at[owner, k], "cols", to)
 
     def xo_copy(to, owner):
@@ -87,8 +95,10 @@
     def above_ok(s):
         return (z + s < depth) & (z >= half)
 
+    fetches[0].wait()
+
     for k in range(chunks):
-        lines = pl.ds(k * LANES, LANES)
+        lines = pl.ds(k * PIECE, PIECE)
         unit = normalize(be[lines, :])
         col_buf[r, lines, :] = unit
         row_buf[c, lines, :] = unit
@@ -106,6 +116,8 @@
         hop(r, k, core_sem, partner).start()
         peers(n_cols, c, lambda p: x_copy(k, p, c).start())
 
+    for fetch in fetches[1:4]:
+        fetch.wait()
     row_ord[c] = bo[...]
     peers(n_cols, c, lambda p: xo_copy(p, c).start())
 
@@ -119,8 +131,13 @@
         meta_s[p, 1:2, :width] = clus[p:p + 1, :]
         meta_s[p, 2:3, :width] = order[p:p + 1, :]
     peers(n_rows, r, lambda p: me_copy(p, r).start())
+    fetches[4].wait()
     sm_s[...] = normalize(se[0])
-    peers(n_rows, r, lambda p: sm_copy(p, r).start())
+
+    @pl.when(z >= half)
+    def _():
+        peers(n_rows, r, lambda p: sm_copy(p, r).start())
+
     meta_r[r] = meta_s[r]
     sm_r[r] = sm_s[r]
     acc[...] = jnp.full(acc.shape, -1.0, jnp.float32)
@@ -170,10 +187,11 @@
 
     def pair(b, k):
         other = (b // 2) * 2 + 1 - core
-        hop(other, k, core_sem, partner).wait_recv()
+        for piece in range(k * ratio, (k + 1) * ratio):
+            hop(other, piece, core_sem, partner).wait_recv()
         scores_of(b, k, True)
         scores_of(other, k, True)
-        if k == chunks - 1:
+        if k == chunks // ratio - 1:
             cm_copy(b, r).start()
             cm_copy(other, r).start()
 
@@ -194,10 +212,23 @@
     peers(n_cols, c, lambda p: xo_copy(p, p).wait_recv())
     peers(n_rows, r, lambda p: me_copy(p, p).wait_recv())
     for k in range(chunks):
+        hop(partner, k, core_sem, partner).wait_recv()
+    for k in range(chunks // ratio):
         scores_of(r, k, False)
-        hop(partner, k, core_sem, partner).wait_recv()
         scores_of(partner, k, False)
 
+    @pl.when(z < half)
+    def _():
+        peers(n_rows, r, lambda p: sm_copy(p, r).start())
+
+    def step(s, carry):
+        for k in range(chunks):
+            forward(s, k)
+            if k % ratio == ratio - 1:
+                pairs(s - 1, k // ratio)
+        return carry
+
+    lax.fori_loop(2, depth, step, 0)
     peers(n_rows, r, lambda p: sm_copy(p, p).wait_recv())
     slots = n_rows * cap
     clus_row = jnp.sum(meta_r[:, 1, :width], axis=0, keepdims=True)
@@ -217,14 +248,7 @@
     rs_r[r] = best
     peers(n_rows, r, lambda p: rs_copy(p, r).start())
 
-    def step(s, carry):
-        for k in range(chunks):
-            forward(s, k)
-            pairs(s - 1, k)
-        return carry
-
-    lax.fori_loop(2, depth, step, 0)
-    for k in range(chunks):
+    for k in range(chunks // ratio):
         pairs(depth - 1, k)
 
     final = jnp.max(acc[...], axis=0, keepdims=True)
@@ -235,27 +259,6 @@
     peers(n_rows, r, lambda p: rs_copy(p, p).wait_recv())
     back = pltpu.roll(rs_r[:, 0, :], lax.rem(width - r * cap, width), 1)
     out_s[0] = back[:, :cap]
-
-    out_b[...] = pm_s[c]
-
-    def returned(p, carry):
-        zp = p // 2
-        low = (z < half) & (zp > z)
-        high = (z >= half) & (zp >= half) & (zp < z)
-
-        @pl.when(low | high)
-        def _():
-            cm_copy(p, p).wait_recv()
-            out_b[...] = jnp.maximum(out_b[...], cm_r[p])
-        return carry
-
-    lax.fori_loop(0, n_rows, returned, 0)
-
-    def merge(p):
-        pm_copy(p, p).wait_recv()
-        out_b[...] = jnp.maximum(out_b[...], pm_r[p])
-
-    peers(n_cols, c, merge)
 
     def sent(b):
         for k in range(chunks):
@@ -309,6 +312,27 @@
 
     peers(n_rows, r, row_sent)
 
+    out_b[...] = pm_s[c]
+
+    def returned(p, carry):
+        zp = p // 2
+        low = (z < half) & (zp > z)
+        high = (z >= half) & (zp >= half) & (zp < z)
+
+        @pl.when(low | high)
+        def _():
+            cm_copy(p, p).wait_recv()
+            out_b[...] = jnp.maximum(out_b[...], cm_r[p])
+        return carry
+
+    lax.fori_loop(0, n_rows, returned, 0)
+
+    def merge(p):
+        pm_copy(p, p).wait_recv()
+        out_b[...] = jnp.maximum(out_b[...], pm_r[p])
+
+    peers(n_cols, c, merge)
+
     def col_sent(p):
         xo_copy(p, c).wait_send()
         pm_copy(p, c).wait_send()
@@ -320,7 +344,7 @@
     block, dim = big_emb.shape
     cap = small_emb.shape[2]
     width = n_rows * cap
-    chunks = block // LANES
+    chunks = block // PIECE
     depth = n_rows // 2
     meta = max(block, width)
     bf16, f32, i32 = jnp.bfloat16, jnp.float32, jnp.int32
@@ -332,9 +356,15 @@
             jax.ShapeDtypeStruct((1, block), f32),
             jax.ShapeDtypeStruct((1, n_rows, cap), f32),
         ),
-        in_specs=[vmem] * 5,
+        in_specs=[pl.BlockSpec(memory_space=pl.ANY)] * 5,
         out_specs=(vmem, vmem),
         scratch_shapes=[
+            pltpu.VMEM(big_emb.shape, bf16),
+            pltpu.VMEM((1, block), i32),
+            pltpu.VMEM(small_emb.shape, bf16),
+            pltpu.VMEM(small_clus.shape, i32),
+            pltpu.VMEM(small_order.shape, i32),
+            dma((5,)),
             pltpu.VMEM((n_rows, block, dim), bf16),
             pltpu.VMEM((n_cols, block, dim), bf16),
             pltpu.VMEM((n_cols, 1, block), i32),
@@ -370,7 +400,7 @@
             dma((n_rows,)),
         ],
         compiler_params=pltpu.CompilerParams(
-            collective_id=0, has_side_effects=True, vmem_limit_bytes=48 * 1024 * 1024
+            collective_id=0, has_side_effects=True, vmem_limit_bytes=60 * 1024 * 1024
         ),
     )(big_emb, big_order.reshape(1, block), small_emb, small_clus, small_order)
     return big.reshape(block), small

time: 48.1 us -> 43.3 us (0.900)
  local copies, waits for them, and re-layouts: 5.12 us -> 1.79 us
  Pallas kernels: 42 us -> 40.7 us
    unnamed x12 -> x6, local copies, waits for them, and re-layouts: 5.12 us -> 1.79 us
    pallas_call x1, Pallas kernels: 42 us -> 40.7 us  [local(): pl.pallas_call(functools.partial(kernel, n_rows, n_cols), out_shape=(jax....]
where the time goes in v2:
time: 43.3 us; the launch traced here: 43.2 us
  Pallas kernels  40.7 us (94%)
  local copies, waits for them, and re-layouts  1.79 us (4%)
  between operations  0.66 us (2%)
    pallas_call x1, Pallas kernels, local(): pl.pallas_call(functools.partial(kernel, n_rows, n_cols), out_shape=(jax....  40.7 us
    unnamed x6, local copies, waits for them, and re-layouts  1.79 us

profile of v2, /device:TPU:0, one launch (start us, length us, event | category | flops | bytes accessed | tf_op | source)
XLA Modules:
  0.0 43.2 jit_solution(17795671441951295919)
XLA Ops:
  0.6 40.7 %shard_map.68 = (f32[1,256]{1,0:T(1,128)}, f32[1,8,16]{2,1,0:T(8,128)}) custom-call(bf16[256,768]{1,0:T(8,128)(2,1)} %be_in.1, s32[1,256]{1,0:T(1,128)} %bitcast.2, bf16[1,8,16,768]{3,2,1,0:T(8,128)(2,1)} %se_in.1, s32[1,8,16]{2,1,0:T(8,128)} %sc_in.1, s32[1,8,16]{2,1,0:T(8,128)} %so_in.1), custom_call_target="tpu_custom_call" | custom-call | tf_op jit(solution)/shard_map/pallas_call | solution.py:353
  41.4 0.0 copy-start
  41.4 0.0 copy-start.1
  41.4 0.6 %copy-done.1 = f32[1,256]{1,0:T(1,128)S(1)} copy-done((f32[1,256]{1,0:T(1,128)S(1)}, f32[1,256]{1,0:T(1,128)}, u32[]{:S(2)}) %copy-start.1) | copy-done | bytes 1048
  42.0 0.6 %copy.9 = f32[256]{0:T(256)} copy(f32[256]{0:T(256)S(1)} %bitcast.3) | data formatting | bytes 2048
  42.6 0.0 copy-done
  42.6 0.6 %copy.10 = f32[1,8,16]{2,1,0:T(8,128)} copy(f32[1,8,16]{2,1,0:T(8,128)S(1)} %copy-done) | data formatting | bytes 1024
Async XLA Ops:
  41.4 1.2 %copy-start = (f32[1,8,16]{2,1,0:T(8,128)S(1)}, f32[1,8,16]{2,1,0:T(8,128)}, u32[]{:S(2)}) copy-start(f32[1,8,16]{2,1,0:T(8,128)} %get-tuple-element.9) | copy-start | bytes 1540
  41.4 0.6 %copy-start.1 = (f32[1,256]{1,0:T(1,128)S(1)}, f32[1,256]{1,0:T(1,128)}, u32[]{:S(2)}) copy-start(f32[1,256]{1,0:T(1,128)} %get-tuple-element.4) | copy-start | bytes 3076

commit v3 on v2

--- a/solution.py
+++ b/solution.py
@@ -8,7 +8,7 @@
 from jax.sharding import PartitionSpec as P
 
 LANES = 128
-PIECE = 64
+PIECE = 32
 MESH = pl.DeviceIdType.MESH
 
 
@@ -24,8 +24,8 @@
 
 def kernel(
     n_rows, n_cols,
-    be_in, bo_in, se_in, sc_in, so_in, out_b, out_s,
-    be, bo, se, sc, so, in_sem, col_buf, row_buf, row_ord, meta_s, meta_r, sm_s, sm_r, acc, pm_s, pm_r, cm_s, cm_r, rs_s, rs_r, pad,
+    be_in, bo_in, se_in, sc_in, so_in, out_b_hbm, out_s_hbm,
+    out_b, out_s, out_sem, be, bo, se, sc, so, in_sem, col_buf, row_buf, row_ord, meta_s, meta_r, sm_s, sm_r, acc, pm_s, pm_r, cm_s, cm_r, rs_s, rs_r, pad,
     recv, up_sem, down_sem, core_sem, x_send, x_recv, xo_send, xo_recv,
     me_send, me_recv, sm_send, sm_recv, rs_send, rs_recv, pm_send, pm_recv, cm_send, cm_recv,
 ):
@@ -39,7 +39,7 @@
     c = lax.axis_index("cols")
     z, core = r // 2, r % 2
     partner = z * 2 + 1 - core
-    depth, half = n_rows // 2, n_rows // 4
+    depth, half = n_rows // 2, max(n_rows // 4 - 1, 0)
     block = be.shape[0]
     chunks = block // PIECE
     ratio = LANES // PIECE
@@ -134,7 +134,7 @@
     fetches[4].wait()
     sm_s[...] = normalize(se[0])
 
-    @pl.when(z >= half)
+    @pl.when(z <= half)
     def _():
         peers(n_rows, r, lambda p: sm_copy(p, r).start())
 
@@ -217,7 +217,7 @@
         scores_of(r, k, False)
         scores_of(partner, k, False)
 
-    @pl.when(z < half)
+    @pl.when(z > half)
     def _():
         peers(n_rows, r, lambda p: sm_copy(p, r).start())
 
@@ -259,6 +259,8 @@
     peers(n_rows, r, lambda p: rs_copy(p, p).wait_recv())
     back = pltpu.roll(rs_r[:, 0, :], lax.rem(width - r * cap, width), 1)
     out_s[0] = back[:, :cap]
+    small_out = pltpu.make_async_copy(out_s, out_s_hbm, out_sem.at[1])
+    small_out.start()
 
     def sent(b):
         for k in range(chunks):
@@ -337,7 +339,11 @@
         xo_copy(p, c).wait_send()
         pm_copy(p, c).wait_send()
 
+    big_out = pltpu.make_async_copy(out_b, out_b_hbm, out_sem.at[0])
+    big_out.start()
     peers(n_cols, c, col_sent)
+    small_out.wait()
+    big_out.wait()
 
 
 def local(n_rows, n_cols, big_emb, big_order, small_emb, small_clus, small_order):
@@ -349,16 +355,19 @@
     meta = max(block, width)
     bf16, f32, i32 = jnp.bfloat16, jnp.float32, jnp.int32
     dma = pltpu.SemaphoreType.DMA
-    vmem = pl.BlockSpec(memory_space=pltpu.VMEM)
+    hbm = pl.BlockSpec(memory_space=pltpu.HBM)
     big, small = pl.pallas_call(
         functools.partial(kernel, n_rows, n_cols),
         out_shape=(
             jax.ShapeDtypeStruct((1, block), f32),
             jax.ShapeDtypeStruct((1, n_rows, cap), f32),
         ),
-        in_specs=[pl.BlockSpec(memory_space=pl.ANY)] * 5,
-        out_specs=(vmem, vmem),
+        in_specs=[hbm] * 5,
+        out_specs=(hbm, hbm),
         scratch_shapes=[
+            pltpu.VMEM((1, block), f32),
+            pltpu.VMEM((1, n_rows, cap), f32),
+            dma((2,)),
             pltpu.VMEM(big_emb.shape, bf16),
             pltpu.VMEM((1, block), i32),
             pltpu.VMEM(small_emb.shape, bf16),

time: 43.3 us -> 41.3 us (0.954)
  Pallas kernels: 40.7 us -> 38.7 us
    pallas_call x1, Pallas kernels: 40.7 us -> 38.7 us  [local(): pl.pallas_call(functools.partial(kernel, n_rows, n_cols), out_shape=(jax....]
where the time goes in v3:
time: 41.3 us; the launch traced here: 41.1 us
  Pallas kernels  38.7 us (94%)
  local copies, waits for them, and re-layouts  1.79 us (4%)
  between operations  0.66 us (2%)
    pallas_call x1, Pallas kernels, local(): pl.pallas_call(functools.partial(kernel, n_rows, n_cols), out_shape=(jax....  38.7 us
    unnamed x6, local copies, waits for them, and re-layouts  1.79 us

profile of v3, /device:TPU:0, one launch (start us, length us, event | category | flops | bytes accessed | tf_op | source)
XLA Modules:
  0.0 41.1 jit_solution(10652544503536325109)
XLA Ops:
  0.6 38.7 %shard_map.68 = (f32[1,256]{1,0:T(1,128)}, f32[1,8,16]{2,1,0:T(8,128)}) custom-call(bf16[256,768]{1,0:T(8,128)(2,1)} %be_in.1, s32[1,256]{1,0:T(1,128)} %bitcast.2, bf16[1,8,16,768]{3,2,1,0:T(8,128)(2,1)} %se_in.1, s32[1,8,16]{2,1,0:T(8,128)} %sc_in.1, s32[1,8,16]{2,1,0:T(8,128)} %so_in.1), custom_call_target="tpu_custom_call" | custom-call | tf_op jit(solution)/shard_map/pallas_call | solution.py:359
  39.3 0.0 copy-start
  39.3 0.0 copy-start.1
  39.3 0.6 %copy-done.1 = f32[1,256]{1,0:T(1,128)S(1)} copy-done((f32[1,256]{1,0:T(1,128)S(1)}, f32[1,256]{1,0:T(1,128)}, u32[]{:S(2)}) %copy-start.1) | copy-done | bytes 1048
  39.9 0.6 %copy.9 = f32[256]{0:T(256)} copy(f32[256]{0:T(256)S(1)} %bitcast.3) | data formatting | bytes 2048
  40.5 0.0 copy-done
  40.5 0.6 %copy.10 = f32[1,8,16]{2,1,0:T(8,128)} copy(f32[1,8,16]{2,1,0:T(8,128)S(1)} %copy-done) | data formatting | bytes 1024
Async XLA Ops:
  39.3 1.2 %copy-start = (f32[1,8,16]{2,1,0:T(8,128)S(1)}, f32[1,8,16]{2,1,0:T(8,128)}, u32[]{:S(2)}) copy-start(f32[1,8,16]{2,1,0:T(8,128)} %get-tuple-element.9) | copy-start | bytes 1540
  39.3 0.6 %copy-start.1 = (f32[1,256]{1,0:T(1,128)S(1)}, f32[1,256]{1,0:T(1,128)}, u32[]{:S(2)}) copy-start(f32[1,256]{1,0:T(1,128)} %get-tuple-element.4) | copy-start | bytes 3076
